TPU v7x, 128 devices: a whole 4x4x4 slice. The times are simulated.
128 devices in a mesh: seq: 8 (over z, y_hi), grp: 16 (over y_lo, x, core).
Axes of the slice: x: 4, y: 4 (y_hi: 2, y_lo: 2; y = y_hi * 2 + y_lo), z: 4, core: 2. Of those that a mesh axis runs over, the one named last changes fastest.
Arguments:
- self_query: bfloat16 [16, 1024, 5120], P('grp', 'seq'), may hold values from -250 to 250
- self_key: bfloat16 [16, 1024, 5120], P('grp', 'seq'), may hold values from -12 to 12
- self_value: bfloat16 [16, 1024, 5120], P('grp', 'seq'), may hold values from -6 to 6
- self_upstream: bfloat16 [16, 1024, 5120], P('grp', 'seq'), may hold values from -6 to 6
- cross_query: bfloat16 [16, 1024, 5120], P('grp', 'seq'), may hold values from -250 to 250
- context_key: bfloat16 [512, 5120], replicated, may hold values from -12 to 12
- context_value: bfloat16 [512, 5120], replicated, may hold values from -6 to 6
- cross_upstream: bfloat16 [16, 1024, 5120], P('grp', 'seq'), may hold values from -6 to 6
Outputs:
- query_grad: bfloat16 [16, 1024, 5120], P('grp', 'seq')
- key_grad: bfloat16 [16, 1024, 5120], P('grp', 'seq')
- value_grad: bfloat16 [16, 1024, 5120], P('grp', 'seq')
- cross_query_grad: bfloat16 [16, 1024, 5120], P('grp', 'seq')
- context_key_grad: float32 [512, 5120], P(None, 'seq')
- context_value_grad: float32 [512, 5120], P(None, 'seq')
All inputs are finite; a program needn't handle non-finite values.
Results may differ from a plain program's by a relative error of at most 0.013.
Values may be sent and summed in bfloat16 or wider, within the bound.
A program may use at most 256 MiB of HBM per device.

v0:
```python
import jax
import jax.numpy as jnp
from jax import lax
from jax.sharding import PartitionSpec as P

HD = 128


def pick_rows(row_count, largest):
    block_rows = min(largest, row_count)
    while row_count % block_rows:
        block_rows = block_rows - 1
    return block_rows


def block_backward(queries, key_in, value_in, upstream):
    row_count, head_count, head_depth = queries.shape
    block_rows = pick_rows(row_count, 512)
    block_count = row_count // block_rows
    piece_rows = pick_rows(block_rows, 128)
    piece_count = block_rows // piece_rows
    scaling = HD ** (-0.5)

    def advance(totals, pieces):
        query_block, upstream_block = pieces
        scores = (
            jnp.einsum("nhe,mhe->hnm", query_block, key_in, preferred_element_type=jnp.float32)
            * scaling
        )
        weights = jax.nn.softmax(scores, axis=-1)
        rounded = weights.astype(jnp.bfloat16)
        output = jnp.einsum("hnm,mhe->nhe", rounded, value_in, preferred_element_type=jnp.float32)
        row_inner = jnp.sum(upstream_block.astype(jnp.float32) * output, axis=-1)
        grad_prob = jnp.einsum(
            "nhe,mhe->hnm", upstream_block, value_in, preferred_element_type=jnp.float32
        )
        grad_score = (
            weights * (grad_prob - jnp.transpose(row_inner)[:, :, None]) * scaling
        ).astype(jnp.bfloat16)
        query_grad = jnp.einsum(
            "hnm,mhe->nhe", grad_score, key_in, preferred_element_type=jnp.float32
        ).astype(jnp.bfloat16)
        score_split = grad_score.reshape(head_count, piece_count, piece_rows, grad_score.shape[2])
        weight_split = rounded.reshape(head_count, piece_count, piece_rows, rounded.shape[2])
        query_split = query_block.reshape(piece_count, piece_rows, head_count, head_depth)
        upstream_split = upstream_block.reshape(piece_count, piece_rows, head_count, head_depth)
        key_terms = jnp.einsum(
            "hgnm,gnhe->gmhe", score_split, query_split, preferred_element_type=jnp.float32
        )
        value_terms = jnp.einsum(
            "hgnm,gnhe->gmhe", weight_split, upstream_split, preferred_element_type=jnp.float32
        )
        key_sum = totals[0] + jnp.sum(key_terms, axis=0)
        value_sum = totals[1] + jnp.sum(value_terms, axis=0)
        return ((key_sum, value_sum), query_grad)

    zero_sum = jnp.zeros(key_in.shape, jnp.float32)
    blocked = (
        queries.reshape(block_count, block_rows, head_count, head_depth),
        upstream.reshape(block_count, block_rows, head_count, head_depth),
    )
    running, query_grads = lax.scan(advance, (zero_sum, zero_sum), blocked)
    return (query_grads.reshape(row_count, head_count, head_depth), running[0], running[1])


def shards(
    self_query,
    self_key,
    self_value,
    self_upstream,
    cross_query,
    context_key,
    context_value,
    cross_upstream,
):
    token_count = self_query.shape[1]
    full_width = self_query.shape[2]
    head_count = full_width // HD
    text_rows = context_key.shape[0]
    seq_count = lax.axis_size("seq")
    group_heads = head_count // seq_count

    def to_heads(tensor):
        return tensor.reshape(token_count, head_count, HD)

    def to_groups(tensor):
        return tensor.reshape(token_count, seq_count, group_heads, HD)

    pieces = (
        lax.all_to_all(to_groups(self_query[0]), "seq", split_axis=1, concat_axis=0, tiled=True),
        lax.all_to_all(to_groups(self_key[0]), "seq", split_axis=1, concat_axis=0, tiled=True),
        lax.all_to_all(to_groups(self_value[0]), "seq", split_axis=1, concat_axis=0, tiled=True),
        lax.all_to_all(to_groups(self_upstream[0]), "seq", split_axis=1, concat_axis=0, tiled=True),
    )
    rows = pieces[0].shape[0]
    items = pieces[0].shape[2]

    def flat(tensor):
        return tensor.reshape(rows, items, HD)

    query_part, key_part, value_part = block_backward(
        flat(pieces[0]), flat(pieces[1]), flat(pieces[2]), flat(pieces[3])
    )
    shape_back = (rows, 1, items, HD)
    query_grad, key_grad, value_grad = (
        lax.all_to_all(
            query_part.reshape(shape_back), "seq", split_axis=0, concat_axis=1, tiled=True
        ),
        lax.all_to_all(
            key_part.astype(jnp.bfloat16).reshape(shape_back),
            "seq",
            split_axis=0,
            concat_axis=1,
            tiled=True,
        ),
        lax.all_to_all(
            value_part.astype(jnp.bfloat16).reshape(shape_back),
            "seq",
            split_axis=0,
            concat_axis=1,
            tiled=True,
        ),
    )
    columns = full_width // seq_count
    offset = lax.axis_index("seq") * columns
    context_heads = context_key.reshape(text_rows, head_count, HD)
    value_heads = context_value.reshape(text_rows, head_count, HD)
    cross_grad, context_keys_part, context_values_part = block_backward(
        to_heads(cross_query[0]), context_heads, value_heads, to_heads(cross_upstream[0])
    )
    key_partial = context_keys_part.reshape(text_rows, full_width)
    value_partial = context_values_part.reshape(text_rows, full_width)
    key_whole, value_whole = lax.psum((key_partial, value_partial), ("seq", "grp"))
    key_total = lax.dynamic_slice_in_dim(key_whole, offset, columns, 1)
    value_total = lax.dynamic_slice_in_dim(value_whole, offset, columns, 1)
    shape_out = (1, token_count, full_width)
    return (
        query_grad.reshape(shape_out),
        key_grad.reshape(shape_out),
        value_grad.reshape(shape_out),
        cross_grad.reshape(shape_out),
        key_total,
        value_total,
    )


def solution(mesh):
    return jax.shard_map(
        shards,
        mesh=mesh,
        in_specs=(
            P("grp", "seq", None),
            P("grp", "seq", None),
            P("grp", "seq", None),
            P("grp", "seq", None),
            P("grp", "seq", None),
            P(),
            P(),
            P("grp", "seq", None),
        ),
        out_specs=(
            P("grp", "seq", None),
            P("grp", "seq", None),
            P("grp", "seq", None),
            P("grp", "seq", None),
            P(None, "seq"),
            P(None, "seq"),
        ),
        check_vma=False,
    )
```

profile of v0, /device:TPU:1, one launch (start us, length us, event | category | flops | bytes accessed | tf_op | source)
XLA Modules:
  0.0 414.7 jit_solution(14000686213218465211)
XLA Ops:
  7.2 2.5 copy.98
  9.7 8.5 %all-to-all-start = ((bf16[128,8,5,128]{0,3,2,1:T(8,128)(2,1)}), bf16[128,8,5,128]{0,3,2,1:T(8,128)(2,1)S(1)}, u32[]{:S(2)}, u32[]{:S(2)}) async-start(bf16[128,8,5,128]{0,3,2,1:T(8,128)(2,1)} %bitcast), calls=%async_computation | async-start | bytes 2621440 | tf_op jit(solution)/shard_map/all_to_all | solution.py:90
  21.4 7.9 %copy.145 = bf16[512,5120]{0,1:T(8,128)(2,1)} copy(bf16[512,5120]{1,0:T(8,128)(2,1)} %param.15) | data formatting | bytes 10485760 | tf_op jit(solution)/shard_map/reshape | solution.py:126
  29.3 10.0 %fusion.36 = (f32[40,128]{1,0:T(8,128)S(1)}, f32[40,128,512]{2,1,0:T(8,128)}) fusion(bf16[128,40,128]{0,2,1:T(8,128)(2,1)S(1)} %bitcast.198, bf16[512,40,128]{0,2,1:T(8,128)(2,1)} %bitcast.196), kind=kOutput, calls=%fused_computation.42 | convolution fusion | flops 678953472 | bytes 17059840 | tf_op jit(solution)/shard_map/while/body/eval_jaxpr/sub | solution.py:30
  39.3 6.6 %all-to-all-start.1 = ((bf16[128,8,5,128]{0,3,2,1:T(8,128)(2,1)}), bf16[128,8,5,128]{0,3,2,1:T(8,128)(2,1)}, u32[]{:S(2)}, u32[]{:S(2)}) async-start(bf16[128,8,5,128]{0,3,2,1:T(8,128)(2,1)} %bitcast.211), calls=%async_computation.1 | async-start | bytes 2621440 | tf_op jit(solution)/shard_map/all_to_all | solution.py:91
  46.0 7.3 %fusion.26 = bf16[40,128,512]{2,1,0:T(8,128)(2,1)} fusion(f32[40,128,512]{2,1,0:T(8,128)} %get-tuple-element.175, f32[40,128]{1,0:T(8,128)S(1)} %get-tuple-element.174), kind=kLoop, calls=%fused_computation.31 | loop fusion | flops 5242880 | bytes 15749120 | tf_op jit(solution)/shard_map/while/body/eval_jaxpr/convert_element_type | solution.py:31
  53.3 2.4 copy.102
  55.7 2.4 copy.104
  59.9 8.0 %copy.146 = bf16[512,5120]{0,1:T(8,128)(2,1)} copy(bf16[512,5120]{1,0:T(8,128)(2,1)} %param.16) | data formatting | bytes 10485760 | tf_op jit(solution)/shard_map/reshape | solution.py:127
  67.8 5.6 %fusion.27 = f32[128,40]{0,1:T(8,128)S(1)} fusion(bf16[128,40,128]{0,2,1:T(8,128)(2,1)S(1)} %bitcast.202, bf16[40,128,512]{2,1,0:T(8,128)(2,1)} %fusion.26, bf16[512,40,128]{0,2,1:T(8,128)(2,1)} %bitcast.207), kind=kOutput, calls=%fused_computation.33 | convolution fusion | flops 673049600 | bytes 11816960 | tf_op jit(solution)/shard_map/while/body/eval_jaxpr/hnm,mhe->nhe/dot_general | solution.py:32
  73.4 6.7 %all-to-all-start.2 = ((bf16[128,8,5,128]{0,3,2,1:T(8,128)(2,1)}), bf16[128,8,5,128]{0,3,2,1:T(8,128)(2,1)}, u32[]{:S(2)}, u32[]{:S(2)}) async-start(bf16[128,8,5,128]{0,3,2,1:T(8,128)(2,1)} %bitcast.212), calls=%async_computation.2 | async-start | bytes 2621440 | tf_op jit(solution)/shard_map/all_to_all | solution.py:93
  80.1 8.3 %multiply_convert_fusion.1 = bf16[40,128,512]{2,1,0:T(8,128)(2,1)} fusion(f32[40,128]{1,0:T(8,128)S(1)} %bitcast.223, f32[40,128,512]{2,1,0:T(8,128)} %get-tuple-element.175, f32[40,128]{1,0:T(8,128)S(1)} %get-tuple-element.174, bf16[128,40,128]{0,2,1:T(8,128)(2,1)S(1)} %bitcast.203, bf16[512,40,128]{0,2,1:T(8,128)(2,1)} %bitcast.208), kind=kOutput, calls=%fused_computation.25 | convolution fusion | flops 684195840 | bytes 22323200 | tf_op jit(solution)/shard_map/while/body/eval_jaxpr/nhe,mhe->hnm/dot_general | solution.py:34
  88.4 9.4 %all-to-all-done.2 = bf16[128,8,5,128]{0,3,2,1:T(8,128)(2,1)} async-done(((bf16[128,8,5,128]{0,3,2,1:T(8,128)(2,1)}), bf16[128,8,5,128]{0,3,2,1:T(8,128)(2,1)}, u32[]{:S(2)}, u32[]{:S(2)}) %all-to-all-start.2) | async-done | bytes 1310752 | tf_op jit(solution)/shard_map/all_to_all | solution.py:93
  97.9 4.5 %all-to-all-start.3 = ((bf16[128,8,5,128]{0,3,2,1:T(8,128)(2,1)}), bf16[128,8,5,128]{0,3,2,1:T(8,128)(2,1)}, u32[]{:S(2)}, u32[]{:S(2)}) async-start(bf16[128,8,5,128]{0,3,2,1:T(8,128)(2,1)} %bitcast.210), calls=%async_computation.3 | async-start | bytes 2621440 | tf_op jit(solution)/shard_map/all_to_all | solution.py:92
  102.6 7.8 %fusion.37 = f32[40,512,128]{1,2,0:T(8,128)} fusion(bf16[128,40,128]{0,2,1:T(8,128)(2,1)S(1)} %bitcast.199, bf16[40,128,512]{2,1,0:T(8,128)(2,1)} %multiply_convert_fusion.1), kind=kOutput, calls=%fused_computation.43 | convolution fusion | flops 671088640 | bytes 17039360 | tf_op jit(solution)/shard_map/while/body/eval_jaxpr/hgnm,gnhe->gmhe/dot_general | solution.py:47
  110.4 11.5 %copy.127 = f32[512,5120]{1,0:T(8,128)} copy(f32[512,5120]{0,1:T(8,128)} %bitcast.193) | data formatting | bytes 20971520 | tf_op jit(solution)/shard_map/reshape | solution.py:131
  121.9 8.0 %fusion.38 = f32[40,512,128]{1,2,0:T(8,128)} fusion(bf16[128,40,128]{0,2,1:T(8,128)(2,1)S(1)} %bitcast.204, bf16[40,128,512]{2,1,0:T(8,128)(2,1)} %fusion.26), kind=kOutput, calls=%fused_computation.44 | convolution fusion | flops 671088640 | bytes 17039360 | tf_op jit(solution)/shard_map/while/body/eval_jaxpr/hgnm,gnhe->gmhe/dot_general | solution.py:50
  129.8 11.5 %copy.128 = f32[512,5120]{1,0:T(8,128)} copy(f32[512,5120]{0,1:T(8,128)} %bitcast.192) | data formatting | bytes 20971520 | tf_op jit(solution)/shard_map/reshape | solution.py:132
  144.1 2.4 copy.101
  146.5 2.4 copy.103
  152.1 76.3 %while.3 = (s32[]{:T(128)}, f32[1024,5,128]{0,2,1:T(8,128)}, f32[1024,5,128]{0,2,1:T(8,128)}, bf16[2,512,5,128]{3,1,0,2:T(8,128)(2,1)}, bf16[2,512,5,128]{3,1,0,...) while((s32[]{:T(128)}, f32[1024,5,128]{0,2,1:T(8,128)}, ...), condition=%wide.region_4.0_spmd.clone, body=%wide.region_0.4_spmd.clone.sunk | while | flops 4056676864 | bytes 158648704 | solution.py:62
  153.5 8.6 %fusion.92 = (f32[5,512]{1,0:T(8,128)S(1)}, f32[5,512,1024]{2,1,0:T(8,128)}) fusion(bf16[1024,5,128]{2,0,1:T(8,128)(2,1)} %get-tuple-element.260, bf16[1,512,5,128]{3,1,0,2:T(8,128)(2,1)S(1)} %get-tuple-element.231), kind=kOutput, calls=%fused_computation.41.clone.1 | convolution fusion | flops 678953984 | bytes 12462080 | tf_op jit(solution)/shard_map/while/body/eval_jaxpr/sub | solution.py:30
  162.1 5.8 %fusion.93 = bf16[5,512,1024]{2,1,0:T(8,128)(2,1)S(1)} fusion(f32[5,512,1024]{2,1,0:T(8,128)} %get-tuple-element.232, f32[5,512]{1,0:T(8,128)S(1)} %get-tuple-element.233), kind=kLoop, calls=%fused_computation.7.clone.1 | loop fusion | flops 5242880 | bytes 15738880 | tf_op jit(solution)/shard_map/while/body/eval_jaxpr/convert_element_type | solution.py:31
  170.3 7.0 %multiply_convert_fusion.3 = bf16[5,512,1024]{2,1,0:T(8,128)(2,1)} fusion(f32[5,512]{1,0:T(8,128)S(1)} %bitcast.224, f32[5,512,1024]{2,1,0:T(8,128)} %get-tuple-element.232, f32[5,512]{1,0:T(8,128)S(1)} %get-tuple-element.233, bf16[1024,5,128]{0,2,1:T(8,128)(2,1)S(1)} %copy-done.7, bf16[1,512,5,128]{3,1,0,2:T(8,128)(2,1)S(1)} %get-tuple-element.234), kind=kOutput, calls=%fused_computation.1.clone.1 | convolution fusion | flops 684195840 | bytes 17715200 | tf_op jit(solution)/shard_map/while/body/eval_jaxpr/nhe,mhe->hnm/dot_general | solution.py:34
  177.3 5.3 %bitcast_add_fusion.4 = f32[1024,5,128]{0,2,1:T(8,128)} fusion(f32[1024,5,128]{0,2,1:T(8,128)} %get-tuple-element.246, bf16[4,128,5,128]{3,1,0,2:T(8,128)(2,1)S(1)} %bitcast.195, bf16[5,4,128,1024]{3,2,1,0:T(8,128)(2,1)} %bitcast.189, pred[]{:T(512)S(6)} %compare.3), kind=kOutput, calls=%fused_computation.9.clone.1 | convolution fusion | flops 672399360 | bytes 11141121 | tf_op jit(solution)/shard_map/while/body/eval_jaxpr/hgnm,gnhe->gmhe/dot_general | solution.py:47
  182.7 2.5 bitcast_add_fusion.5
  190.7 8.5 %fusion.92 = (f32[5,512]{1,0:T(8,128)S(1)}, f32[5,512,1024]{2,1,0:T(8,128)}) fusion(bf16[1024,5,128]{2,0,1:T(8,128)(2,1)} %get-tuple-element.260, bf16[1,512,5,128]{3,1,0,2:T(8,128)(2,1)S(1)} %get-tuple-element.231), kind=kOutput, calls=%fused_computation.41.clone.1 | convolution fusion | flops 678953984 | bytes 12462080 | tf_op jit(solution)/shard_map/while/body/eval_jaxpr/sub | solution.py:30
  199.2 5.8 %fusion.93 = bf16[5,512,1024]{2,1,0:T(8,128)(2,1)S(1)} fusion(f32[5,512,1024]{2,1,0:T(8,128)} %get-tuple-element.232, f32[5,512]{1,0:T(8,128)S(1)} %get-tuple-element.233), kind=kLoop, calls=%fused_computation.7.clone.1 | loop fusion | flops 5242880 | bytes 15738880 | tf_op jit(solution)/shard_map/while/body/eval_jaxpr/convert_element_type | solution.py:31
  207.4 7.2 %multiply_convert_fusion.3 = bf16[5,512,1024]{2,1,0:T(8,128)(2,1)} fusion(f32[5,512]{1,0:T(8,128)S(1)} %bitcast.224, f32[5,512,1024]{2,1,0:T(8,128)} %get-tuple-element.232, f32[5,512]{1,0:T(8,128)S(1)} %get-tuple-element.233, bf16[1024,5,128]{0,2,1:T(8,128)(2,1)S(1)} %copy-done.7, bf16[1,512,5,128]{3,1,0,2:T(8,128)(2,1)S(1)} %get-tuple-element.234), kind=kOutput, calls=%fused_computation.1.clone.1 | convolution fusion | flops 684195840 | bytes 17715200 | tf_op jit(solution)/shard_map/while/body/eval_jaxpr/nhe,mhe->hnm/dot_general | solution.py:34
  214.6 6.2 %bitcast_add_fusion.4 = f32[1024,5,128]{0,2,1:T(8,128)} fusion(f32[1024,5,128]{0,2,1:T(8,128)} %get-tuple-element.246, bf16[4,128,5,128]{3,1,0,2:T(8,128)(2,1)S(1)} %bitcast.195, bf16[5,4,128,1024]{3,2,1,0:T(8,128)(2,1)} %bitcast.189, pred[]{:T(512)S(6)} %compare.3), kind=kOutput, calls=%fused_computation.9.clone.1 | convolution fusion | flops 672399360 | bytes 11141121 | tf_op jit(solution)/shard_map/while/body/eval_jaxpr/hgnm,gnhe->gmhe/dot_general | solution.py:47
  220.8 4.7 %bitcast_add_fusion.5 = f32[1024,5,128]{0,2,1:T(8,128)} fusion(f32[1024,5,128]{0,2,1:T(8,128)} %get-tuple-element.247, bf16[4,128,5,128]{3,1,0,2:T(8,128)(2,1)S(1)} %bitcast.194, bf16[5,4,128,1024]{3,2,1,0:T(8,128)(2,1)S(1)} %bitcast.188, pred[]{:T(512)S(6)} %compare.3), kind=kOutput, calls=%fused_computation.8.clone.1 | convolution fusion | flops 672399360 | bytes 11141121 | tf_op jit(solution)/shard_map/while/body/eval_jaxpr/hgnm,gnhe->gmhe/dot_general | solution.py:50
  225.6 1.8 fusion.95
  228.4 3.6 copy.110
  232.0 6.9 %all-to-all-start.4 = ((bf16[1024,1,5,128]{3,2,1,0:T(8,128)(2,1)}), bf16[1024,1,5,128]{3,2,1,0:T(8,128)(2,1)}, u32[]{:S(2)}, u32[]{:S(2)}) async-start(bf16[1024,1,5,128]{3,2,1,0:T(8,128)(2,1)} %copy.110), calls=%async_computation.4 | async-start | bytes 4194304 | tf_op jit(solution)/shard_map/all_to_all | solution.py:106
  238.9 3.1 copy.113
  242.0 23.9 %all-to-all-done.4 = bf16[1024,1,5,128]{3,2,1,0:T(8,128)(2,1)} async-done(((bf16[1024,1,5,128]{3,2,1,0:T(8,128)(2,1)}), bf16[1024,1,5,128]{3,2,1,0:T(8,128)(2,1)}, u32[]{:S(2)}, u32[]{:S(2)}) %all-to-all-start.4) | async-done | bytes 1310752 | tf_op jit(solution)/shard_map/all_to_all | solution.py:106
  265.9 5.6 %all-to-all-start.5 = ((bf16[1024,1,5,128]{3,2,1,0:T(8,128)(2,1)}), bf16[1024,1,5,128]{3,2,1,0:T(8,128)(2,1)}, u32[]{:S(2)}, u32[]{:S(2)}) async-start(bf16[1024,1,5,128]{3,2,1,0:T(8,128)(2,1)} %bitcast.206), calls=%async_computation.5 | async-start | bytes 4194304 | tf_op jit(solution)/shard_map/all_to_all | solution.py:109
  271.4 3.1 copy.116
  274.5 24.0 %all-to-all-done.5 = bf16[1024,1,5,128]{3,2,1,0:T(8,128)(2,1)} async-done(((bf16[1024,1,5,128]{3,2,1,0:T(8,128)(2,1)}), bf16[1024,1,5,128]{3,2,1,0:T(8,128)(2,1)}, u32[]{:S(2)}, u32[]{:S(2)}) %all-to-all-start.5) | async-done | bytes 1310752 | tf_op jit(solution)/shard_map/all_to_all | solution.py:109
  298.5 5.5 %all-to-all-start.6 = ((bf16[1024,1,5,128]{3,2,1,0:T(8,128)(2,1)}), bf16[1024,1,5,128]{3,2,1,0:T(8,128)(2,1)S(1)}, u32[]{:S(2)}, u32[]{:S(2)}) async-start(bf16[1024,1,5,128]{3,2,1,0:T(8,128)(2,1)} %bitcast.205), calls=%async_computation.6 | async-start | bytes 4194304 | tf_op jit(solution)/shard_map/all_to_all | solution.py:116
  304.0 5.6 %convolution_convert_fusion.1 = bf16[40,128,128]{1,2,0:T(8,128)(2,1)S(1)} fusion(bf16[40,128,512]{2,1,0:T(8,128)(2,1)} %multiply_convert_fusion.1, bf16[512,40,128]{0,2,1:T(8,128)(2,1)} %bitcast.197), kind=kOutput, calls=%fused_computation.36 | convolution fusion | flops 671744000 | bytes 11796480 | tf_op jit(solution)/shard_map/while/body/eval_jaxpr/hnm,mhe->nhe/dot_general | solution.py:40
  311.1 1.8 copy.111
  314.3 2.4 copy.129
  316.8 1.8 copy.114
  320.0 2.4 copy.130
  322.5 14.6 %all-to-all-done.6 = bf16[1024,1,5,128]{3,2,1,0:T(8,128)(2,1)S(1)} async-done(((bf16[1024,1,5,128]{3,2,1,0:T(8,128)(2,1)}), bf16[1024,1,5,128]{3,2,1,0:T(8,128)(2,1)S(1)}, u32[]{:S(2)}, u32[]{:S(2)}) %all-to-all-start.6) | async-done | bytes 1310752 | tf_op jit(solution)/shard_map/all_to_all | solution.py:116
  339.5 65.0 %all-reduce.3.cloned.1.call-done = (f32[512,5120]{1,0:T(8,128)}, f32[512,5120]{1,0:T(8,128)}) async-done(((f32[512,5120]{1,0:T(8,128)}, f32[512,5120]{1,0:T(8,128)}), (f32[512,5120]{1,0:T(8,128)}, f32[512,5120]{1,0:T(8,128)})) %all-reduce.3.cloned.1.call-update) | async-done | bytes 20971536 | tf_op jit(solution)/shard_map/psum | solution.py:133
  404.4 3.4 constant_dynamic-slice_fusion.2
  (75 shorter events, 30.5 us)
Async XLA Ops:
  7.2 11.0 %copy-start.5 = (bf16[1,128,5120]{2,1,0:T(8,128)(2,1)S(1)}, bf16[1,128,5120]{2,1,0:T(8,128)(2,1)}, u32[]{:S(2)}) copy-start(bf16[1,128,5120]{2,1,0:T(8,128)(2,1)} %param.11) | copy-start | bytes 3932164
  9.7 29.6 %all-to-all-start = ((bf16[128,8,5,128]{0,3,2,1:T(8,128)(2,1)}), bf16[128,8,5,128]{0,3,2,1:T(8,128)(2,1)S(1)}, u32[]{:S(2)}, u32[]{:S(2)}) async-start(bf16[128,8,5,128]{0,3,2,1:T(8,128)(2,1)} %bitcast), calls=%async_computation | async-start | bytes 2621440 | tf_op jit(solution)/shard_map/all_to_all | solution.py:90
  39.3 13.9 %copy-start.3 = (bf16[128,8,5,128]{0,3,2,1:T(8,128)(2,1)}, bf16[128,8,5,128]{0,3,2,1:T(8,128)(2,1)S(1)}, u32[]{:S(2)}) copy-start(bf16[128,8,5,128]{0,3,2,1:T(8,128)(2,1)S(1)} %all-to-all-done) | copy-start | bytes 3932164
  39.3 34.1 %all-to-all-start.1 = ((bf16[128,8,5,128]{0,3,2,1:T(8,128)(2,1)}), bf16[128,8,5,128]{0,3,2,1:T(8,128)(2,1)}, u32[]{:S(2)}, u32[]{:S(2)}) async-start(bf16[128,8,5,128]{0,3,2,1:T(8,128)(2,1)} %bitcast.211), calls=%async_computation.1 | async-start | bytes 2621440 | tf_op jit(solution)/shard_map/all_to_all | solution.py:91
  73.4 24.4 %all-to-all-start.2 = ((bf16[128,8,5,128]{0,3,2,1:T(8,128)(2,1)}), bf16[128,8,5,128]{0,3,2,1:T(8,128)(2,1)}, u32[]{:S(2)}, u32[]{:S(2)}) async-start(bf16[128,8,5,128]{0,3,2,1:T(8,128)(2,1)} %bitcast.212), calls=%async_computation.2 | async-start | bytes 2621440 | tf_op jit(solution)/shard_map/all_to_all | solution.py:93
  97.9 51.0 %all-to-all-start.3 = ((bf16[128,8,5,128]{0,3,2,1:T(8,128)(2,1)}), bf16[128,8,5,128]{0,3,2,1:T(8,128)(2,1)}, u32[]{:S(2)}, u32[]{:S(2)}) async-start(bf16[128,8,5,128]{0,3,2,1:T(8,128)(2,1)} %bitcast.210), calls=%async_computation.3 | async-start | bytes 2621440 | tf_op jit(solution)/shard_map/all_to_all | solution.py:92
  102.4 302.1 %all-reduce.3.cloned.1.call-start = ((), (), s32[]{:S(2)}) async-start(), calls=%async_computation.7 | async-start | bytes 41943040 | tf_op jit(solution)/shard_map/psum | solution.py:133
  141.3 1.3 copy-start.4
  162.1 5.8 %copy-start.7 = (bf16[1024,5,128]{0,2,1:T(8,128)(2,1)S(1)}, bf16[1024,5,128]{0,2,1:T(8,128)(2,1)}, u32[]{:S(2)}) copy-start(bf16[1024,5,128]{0,2,1:T(8,128)(2,1)} %get-tuple-element.262) | copy-start | bytes 3932164 | tf_op jit(solution)/shard_map/while
  168.0 2.4 copy-start
  177.3 5.3 %slice-start = ((s8[5242880]{0:T(1024)(128)(4,1)}), s8[1048576]{0:T(1024)(128)(4,1)S(1)}, s32[]{:S(2)}) async-start(s8[5242880]{0:T(1024)(128)(4,1)} %bitcast.186), calls=%async_computation.8 | async-start | bytes 2097152 | tf_op jit(solution)/shard_map/while
  177.3 5.3 %slice-start.1 = ((s8[5242880]{0:T(1024)(128)(4,1)}), s8[4194304]{0:T(1024)(128)(4,1)S(1)}, s32[]{:S(2)}) async-start(s8[5242880]{0:T(1024)(128)(4,1)} %bitcast.186), calls=%async_computation.9 | async-start | bytes 8388608 | tf_op jit(solution)/shard_map/while
  177.3 7.9 %slice-start.2 = ((s8[5242880]{0:T(1024)(128)(4,1)}), s8[4194304]{0:T(1024)(128)(4,1)S(1)}, s32[]{:S(2)}) async-start(s8[5242880]{0:T(1024)(128)(4,1)} %bitcast.190), calls=%async_computation.10 | async-start | bytes 8388608 | tf_op jit(solution)/shard_map/while
  182.7 2.6 slice-start.3
  182.7 2.5 copy-start.6
  182.7 3.8 copy-start.8
  188.2 1.1 copy-start.9
  199.2 5.8 %copy-start.7 = (bf16[1024,5,128]{0,2,1:T(8,128)(2,1)S(1)}, bf16[1024,5,128]{0,2,1:T(8,128)(2,1)}, u32[]{:S(2)}) copy-start(bf16[1024,5,128]{0,2,1:T(8,128)(2,1)} %get-tuple-element.262) | copy-start | bytes 3932164 | tf_op jit(solution)/shard_map/while
  205.0 2.4 copy-start
  214.6 6.2 %slice-start = ((s8[5242880]{0:T(1024)(128)(4,1)}), s8[1048576]{0:T(1024)(128)(4,1)S(1)}, s32[]{:S(2)}) async-start(s8[5242880]{0:T(1024)(128)(4,1)} %bitcast.186), calls=%async_computation.8 | async-start | bytes 2097152 | tf_op jit(solution)/shard_map/while
  214.6 6.2 %slice-start.1 = ((s8[5242880]{0:T(1024)(128)(4,1)}), s8[4194304]{0:T(1024)(128)(4,1)S(1)}, s32[]{:S(2)}) async-start(s8[5242880]{0:T(1024)(128)(4,1)} %bitcast.186), calls=%async_computation.9 | async-start | bytes 8388608 | tf_op jit(solution)/shard_map/while
  214.6 11.0 %slice-start.2 = ((s8[5242880]{0:T(1024)(128)(4,1)}), s8[4194304]{0:T(1024)(128)(4,1)S(1)}, s32[]{:S(2)}) async-start(s8[5242880]{0:T(1024)(128)(4,1)} %bitcast.190), calls=%async_computation.10 | async-start | bytes 8388608 | tf_op jit(solution)/shard_map/while
  220.7 4.8 %slice-start.3 = ((s8[5242880]{0:T(1024)(128)(4,1)}), s8[1048576]{0:T(1024)(128)(4,1)S(1)}, s32[]{:S(2)}) async-start(s8[5242880]{0:T(1024)(128)(4,1)} %bitcast.190), calls=%async_computation.11 | async-start | bytes 2097152 | tf_op jit(solution)/shard_map/while
  220.8 4.8 %copy-start.6 = (bf16[1024,5,128]{2,0,1:T(8,128)(2,1)S(1)}, bf16[1024,5,128]{2,0,1:T(8,128)(2,1)}, u32[]{:S(2)}) copy-start(bf16[1024,5,128]{2,0,1:T(8,128)(2,1)} %get-tuple-element.260) | copy-start | bytes 3932164 | tf_op jit(solution)/shard_map/while
  220.8 4.8 %copy-start.8 = (bf16[2,512,5,128]{3,1,0,2:T(8,128)(2,1)S(1)}, bf16[2,512,5,128]{3,1,0,2:T(8,128)(2,1)}, u32[]{:S(2)}) copy-start(bf16[2,512,5,128]{3,1,0,2:T(8,128)(2,1)} %get-tuple-element.248) | copy-start | bytes 3932164 | tf_op jit(solution)/shard_map/while
  227.3 1.1 copy-start.9
  232.0 6.9 %copy-start.1 = (f32[1024,5,128]{0,2,1:T(8,128)S(1)}, f32[1024,5,128]{0,2,1:T(8,128)}, u32[]{:S(2)}) copy-start(f32[1024,5,128]{0,2,1:T(8,128)} %get-tuple-element.75) | copy-start | bytes 7864324
  232.0 33.9 %all-to-all-start.4 = ((bf16[1024,1,5,128]{3,2,1,0:T(8,128)(2,1)}), bf16[1024,1,5,128]{3,2,1,0:T(8,128)(2,1)}, u32[]{:S(2)}, u32[]{:S(2)}) async-start(bf16[1024,1,5,128]{3,2,1,0:T(8,128)(2,1)} %copy.110), calls=%async_computation.4 | async-start | bytes 4194304 | tf_op jit(solution)/shard_map/all_to_all | solution.py:106
  242.0 29.4 %copy-start.2 = (f32[1024,5,128]{0,2,1:T(8,128)S(1)}, f32[1024,5,128]{0,2,1:T(8,128)}, u32[]{:S(2)}) copy-start(f32[1024,5,128]{0,2,1:T(8,128)} %get-tuple-element.76) | copy-start | bytes 7864324
  265.9 32.7 %all-to-all-start.5 = ((bf16[1024,1,5,128]{3,2,1,0:T(8,128)(2,1)}), bf16[1024,1,5,128]{3,2,1,0:T(8,128)(2,1)}, u32[]{:S(2)}, u32[]{:S(2)}) async-start(bf16[1024,1,5,128]{3,2,1,0:T(8,128)(2,1)} %bitcast.206), calls=%async_computation.5 | async-start | bytes 4194304 | tf_op jit(solution)/shard_map/all_to_all | solution.py:109
  298.5 38.5 %all-to-all-start.6 = ((bf16[1024,1,5,128]{3,2,1,0:T(8,128)(2,1)}), bf16[1024,1,5,128]{3,2,1,0:T(8,128)(2,1)S(1)}, u32[]{:S(2)}, u32[]{:S(2)}) async-start(bf16[1024,1,5,128]{3,2,1,0:T(8,128)(2,1)} %bitcast.205), calls=%async_computation.6 | async-start | bytes 4194304 | tf_op jit(solution)/shard_map/all_to_all | solution.py:116
Sparse Core Ops, SparseCore 0:
  141.5 262.9 all-reduce.2
where the time goes:
time: 416 us; the launch traced here: 415 us
  waiting for transfers between devices  137 us (33%)
  matrix products  102 us (25%)
  local copies, waits for them, and re-layouts  97.9 us (24%)
  starting transfers between devices  44.4 us (11%)
  other arithmetic  18.9 us (5%)
  between operations  14.2 us (3%)
    psum x1, waiting for transfers between devices, shards(): lax.psum((key_partial, value_partial), ('seq', 'grp'))  65 us
    sub x3, matrix products, advance(): weights = jax.nn.softmax(scores, axis=-1)  27.1 us
    all_to_all x1, waiting for transfers between devices, shards(): lax.all_to_all(key_part.astype(jnp.bfloat16).reshape(shape_back), 'seq',...  24 us
    all_to_all x1, waiting for transfers between devices, shards(): lax.all_to_all(query_part.reshape(shape_back), 'seq', split_axis=0, conca...  23.9 us
    dot_general x3, matrix products, advance(): jnp.einsum('nhe,mhe->hnm', upstream_block, value_in, preferred_element_ty...  22.5 us
    unnamed x20, local copies, waits for them, and re-layouts  21 us
    dot_general x3, matrix products, advance(): jnp.einsum('hgnm,gnhe->gmhe', score_split, query_split, preferred_element...  19.3 us
    convert_element_type x3, other arithmetic, advance(): rounded = weights.astype(jnp.bfloat16)  18.9 us
  transfers between devices with their start and end apart: 8, of which 5 were waited for; matrix products, arithmetic and copies ran while one was open for 50% of the time, Pallas kernels for 0%

commit v1 on v0

v1 whole, which is shorter than its diff:
```python
import functools
import math

import jax
import jax.numpy as jnp
from jax import lax
from jax.experimental import pallas as pl
from jax.experimental.pallas import tpu as pltpu
from jax.sharding import PartitionSpec as P

HD = 128
SEQ = 8
XC = 8
MESH = pl.DeviceIdType.MESH
SCALE = HD ** (-0.5)
EXP2_SCALE = SCALE * math.log2(math.e)
BLOCK = 256


def contract(left, right, left_dim, right_dim):
    return lax.dot_general(
        left, right, (((left_dim,), (right_dim,)), ((), ())), preferred_element_type=jnp.float32
    )


def attend_block(queries, upstream, keys, values):
    scores = contract(keys, queries, 1, 1)
    top = jnp.max(scores, axis=0, keepdims=True)
    raised = jnp.exp2((scores - top) * EXP2_SCALE)
    weights = raised * (1.0 / jnp.sum(raised, axis=0, keepdims=True))
    rounded = weights.astype(jnp.bfloat16)
    grad_prob = contract(values, upstream, 1, 1)
    delta = jnp.sum(rounded.astype(jnp.float32) * grad_prob, axis=0, keepdims=True)
    grad_score = (weights * (grad_prob - delta)).astype(jnp.bfloat16)
    value_grad = contract(rounded, upstream, 1, 0)
    key_grad = contract(grad_score, queries, 1, 0)
    query_grad = contract(keys, grad_score, 0, 0).T * SCALE
    return query_grad, key_grad, value_grad


def kernel(
    sq, sk, sv, su, cq, ck, cv, cu,
    oq, ok, ov, ocq, ock, ocv,
    self_in, cross_in, ctx, self_out, cross_out, part, pieces, turned, turned_in, other_in, gathered,
    key_acc, value_acc,
    in_send, in_recv, x_send, x_recv, ctx_sem, o_send, o_recv, xo_send, xo_recv,
    p_send, p_recv, t_send, t_recv, y_send, y_recv, g_send, g_recv,
):
    seq = lax.axis_index("seq")
    grp = lax.axis_index("grp")
    lane = lax.rem(grp, XC)
    row = lax.div(grp, XC)
    heads = self_in.shape[0]
    tokens = sq.shape[1]
    rows = self_in.shape[2]
    text = part.shape[2]
    text_piece = pieces.shape[3]

    def seq_peer(d):
        return lax.rem(seq + d, SEQ)

    def lane_peer(d):
        return lax.rem(lane + d, XC)

    def at_seq(p):
        return {"seq": p, "grp": grp}

    def at_lane(p):
        return {"seq": seq, "grp": row * XC + p}

    turn_to = {"seq": lane, "grp": row * XC + seq}
    other_row = {"seq": seq, "grp": (1 - row) * XC + lane}

    def columns(owner, h):
        return pl.ds(pl.multiple_of((owner * heads + h) * HD, HD), HD)

    def token_rows(owner):
        return pl.ds(pl.multiple_of(owner * tokens, tokens), tokens)

    def text_rows(owner):
        return pl.ds(pl.multiple_of(owner * text_piece, text_piece), text_piece)

    def remote(src, dst, send, recv, where):
        pltpu.make_async_remote_copy(
            src_ref=src, dst_ref=dst, send_sem=send, recv_sem=recv, device_id=where, device_id_type=MESH
        ).start()

    def local(src, dst, sem):
        pltpu.make_async_copy(src, dst, sem).start()

    def drain(ref, sem):
        pltpu.make_async_copy(ref, ref, sem).wait()

    def load_ctx(h, carry):
        local(ck.at[:, columns(lane, h)], ctx.at[0, h], ctx_sem)
        local(cv.at[:, columns(lane, h)], ctx.at[1, h], ctx_sem)
        return carry

    lax.fori_loop(0, heads, load_ctx, 0)

    barrier = pltpu.get_barrier_semaphore()

    def greet(d, carry):
        pl.semaphore_signal(barrier, inc=1, device_id=at_seq(seq_peer(d)), device_id_type=MESH)
        pl.semaphore_signal(barrier, inc=1, device_id=at_lane(lane_peer(d)), device_id_type=MESH)
        return carry

    lax.fori_loop(1, SEQ, greet, 0)
    pl.semaphore_signal(barrier, inc=1, device_id=other_row, device_id_type=MESH)

    @pl.when(lane != seq)
    def _():
        pl.semaphore_signal(barrier, inc=1, device_id=turn_to, device_id_type=MESH)
        pl.semaphore_wait(barrier, SEQ + XC)

    @pl.when(lane == seq)
    def _():
        pl.semaphore_wait(barrier, SEQ + XC - 1)

    def send_in(h, carry):
        for a, ref in enumerate((cq, cu)):
            local(ref.at[0, :, columns(lane, h)], cross_in.at[h, a, token_rows(lane)], x_recv.at[h])
        for a, ref in enumerate((sq, sk, sv, su)):
            local(ref.at[0, :, columns(seq, h)], self_in.at[h, a, token_rows(seq)], in_recv.at[h])

        def to_peer(d, inner):
            p = seq_peer(d)
            e = lane_peer(d)
            for a, ref in enumerate((cq, cu)):
                remote(
                    ref.at[0, :, columns(e, h)], cross_in.at[h, a, token_rows(lane)],
                    x_send, x_recv.at[h], at_lane(e),
                )
            for a, ref in enumerate((sq, sk, sv, su)):
                remote(
                    ref.at[0, :, columns(p, h)], self_in.at[h, a, token_rows(seq)],
                    in_send, in_recv.at[h], at_seq(p),
                )
            return inner

        lax.fori_loop(1, SEQ, to_peer, 0)
        return carry

    lax.fori_loop(0, heads, send_in, 0)

    drain(ctx, ctx_sem)

    def cross_head(h, carry):
        drain(cross_in.at[h], x_recv.at[h])
        key_acc[pl.ds(0, text), :] = jnp.zeros((text, HD), jnp.float32)
        value_acc[pl.ds(0, text), :] = jnp.zeros((text, HD), jnp.float32)

        def block(b, inner):
            at = pl.ds(pl.multiple_of(b * BLOCK, BLOCK), BLOCK)
            query_grad, key_grad, value_grad = attend_block(
                cross_in[h, 0, at, :], cross_in[h, 1, at, :], ctx[0, h], ctx[1, h]
            )
            cross_out[h, at, :] = query_grad.astype(jnp.bfloat16)
            key_acc[pl.ds(0, text), :] += key_grad
            value_acc[pl.ds(0, text), :] += value_grad
            return inner

        lax.fori_loop(0, rows // BLOCK, block, 0)
        part[h, 0] = (key_acc[pl.ds(0, text), :] * SCALE).astype(jnp.bfloat16)
        part[h, 1] = value_acc[pl.ds(0, text), :].astype(jnp.bfloat16)

        local(cross_out.at[h, token_rows(lane)], ocq.at[0, :, columns(lane, h)], xo_recv)
        local(part.at[h, :, text_rows(seq)], pieces.at[seq, h], p_recv)

        def to_peer(d, inner):
            p = seq_peer(d)
            e = lane_peer(d)
            remote(
                cross_out.at[h, token_rows(e)], ocq.at[0, :, columns(lane, h)], xo_send, xo_recv, at_lane(e)
            )
            remote(part.at[h, :, text_rows(p)], pieces.at[seq, h], p_send, p_recv, at_seq(p))
            return inner

        lax.fori_loop(1, SEQ, to_peer, 0)
        return carry

    lax.fori_loop(0, heads, cross_head, 0)

    def self_head(h, carry):
        drain(self_in.at[h], in_recv.at[h])
        key_acc[...] = jnp.zeros_like(key_acc)
        value_acc[...] = jnp.zeros_like(value_acc)

        def block(b, inner):
            at = pl.ds(pl.multiple_of(b * BLOCK, BLOCK), BLOCK)
            query_grad, key_grad, value_grad = attend_block(
                self_in[h, 0, at, :], self_in[h, 3, at, :], self_in[h, 1], self_in[h, 2]
            )
            self_out[h, 0, at, :] = query_grad.astype(jnp.bfloat16)
            key_acc[...] += key_grad
            value_acc[...] += value_grad
            return inner

        lax.fori_loop(0, rows // BLOCK, block, 0)
        self_out[h, 1] = (key_acc[...] * SCALE).astype(jnp.bfloat16)
        self_out[h, 2] = value_acc[...].astype(jnp.bfloat16)

        for a, ref in enumerate((oq, ok, ov)):
            local(self_out.at[h, a, token_rows(seq)], ref.at[0, :, columns(seq, h)], o_recv.at[a])

        def to_peer(d, inner):
            p = seq_peer(d)
            for a, ref in enumerate((oq, ok, ov)):
                remote(
                    self_out.at[h, a, token_rows(p)], ref.at[0, :, columns(seq, h)],
                    o_send, o_recv.at[a], at_seq(p),
                )
            return inner

        lax.fori_loop(1, SEQ, to_peer, 0)

        @pl.when(h == 1)
        def _():
            drain(pieces, p_recv)
            total = pieces[0].astype(jnp.float32)
            for i in range(1, SEQ):
                total = total + pieces[i].astype(jnp.float32)
            turned[...] = total

            @pl.when(lane == seq)
            def _():
                local(turned, turned_in, t_recv)

            @pl.when(lane != seq)
            def _():
                remote(turned, turned_in, t_send, t_recv, turn_to)

        @pl.when(h == 2)
        def _():
            drain(turned_in, t_recv)
            remote(turned_in, other_in, y_send, y_recv, other_row)

        @pl.when(h == 3)
        def _():
            drain(other_in, y_recv)
            gathered[lane] = (turned_in[...] + other_in[...]).astype(jnp.bfloat16)

            def to_lane(d, inner):
                remote(gathered.at[lane], gathered.at[lane], g_send, g_recv, at_lane(lane_peer(d)))
                return inner

            lax.fori_loop(1, XC, to_lane, 0)

        return carry

    lax.fori_loop(0, heads, self_head, 0)

    drain(gathered.at[pl.ds(0, XC - 1)], g_recv)
    for h in range(heads):
        for j in range(XC):
            ock[pl.ds(j * text_piece, text_piece), pl.ds(h * HD, HD)] = gathered[j, h, 0].astype(jnp.float32)
            ocv[pl.ds(j * text_piece, text_piece), pl.ds(h * HD, HD)] = gathered[j, h, 1].astype(jnp.float32)

    others = rows - tokens
    drain(self_in.at[:, :, pl.ds(0, others)], in_send)
    drain(cross_in.at[:, :, pl.ds(0, others)], x_send)
    drain(cross_out.at[:, pl.ds(0, others)], xo_send)
    drain(pieces.at[pl.ds(0, SEQ - 1)], p_send)

    @pl.when(lane != seq)
    def _():
        drain(turned, t_send)

    drain(turned_in, y_send)
    drain(gathered.at[pl.ds(0, XC - 1)], g_send)
    drain(self_out.at[:, :, pl.ds(0, others)], o_send)
    drain(ocq, xo_recv)
    for a, ref in enumerate((oq, ok, ov)):
        drain(ref, o_recv.at[a])


def shards(sq, sk, sv, su, cq, ck, cv, cu):
    tokens, width = sq.shape[1], sq.shape[2]
    text = ck.shape[0]
    rows = tokens * SEQ
    heads = width // HD // SEQ
    piece = text // SEQ
    half, full = jnp.bfloat16, jnp.float32
    token_out = jax.ShapeDtypeStruct((1, tokens, width), half)
    text_out = jax.ShapeDtypeStruct((text, width // SEQ), full)
    in_any = pl.BlockSpec(memory_space=pl.ANY)
    in_vmem = pl.BlockSpec(memory_space=pltpu.VMEM)
    dma = pltpu.SemaphoreType.DMA
    return pl.pallas_call(
        kernel,
        out_shape=(token_out,) * 4 + (text_out,) * 2,
        in_specs=[in_any] * 8,
        out_specs=(in_any,) * 4 + (in_vmem,) * 2,
        scratch_shapes=[
            pltpu.VMEM((heads, 4, rows, HD), half),
            pltpu.VMEM((heads, 2, rows, HD), half),
            pltpu.VMEM((2, heads, text, HD), half),
            pltpu.VMEM((heads, 3, rows, HD), half),
            pltpu.VMEM((heads, rows, HD), half),
            pltpu.VMEM((heads, 2, text, HD), half),
            pltpu.VMEM((SEQ, heads, 2, piece, HD), half),
            pltpu.VMEM((heads, 2, piece, HD), full),
            pltpu.VMEM((heads, 2, piece, HD), full),
            pltpu.VMEM((heads, 2, piece, HD), full),
            pltpu.VMEM((XC, heads, 2, piece, HD), half),
            pltpu.VMEM((rows, HD), full),
            pltpu.VMEM((rows, HD), full),
            dma, dma((heads,)), dma, dma((heads,)), dma, dma, dma((3,)), dma, dma,
            dma, dma, dma, dma, dma, dma, dma, dma,
        ],
        compiler_params=pltpu.CompilerParams(
            collective_id=0, has_side_effects=True, vmem_limit_bytes=58 << 20
        ),
        cost_estimate=pl.CostEstimate(flops=10 << 30, bytes_accessed=16 << 20, transcendentals=8 << 20),
    )(sq, sk, sv, su, cq, ck, cv, cu)


def solution(mesh):
    token = P("grp", "seq", None)
    return jax.shard_map(
        shards,
        mesh=mesh,
        in_specs=(token, token, token, token, token, P(), P(), token),
        out_specs=(token, token, token, token, P(None, "seq"), P(None, "seq")),
        check_vma=False,
    )
```

time: 416 us -> 163 us (0.39)
  the two profiles are of different devices: /device:TPU:1 before, /device:TPU:6 now
where the time goes in v1:
time: 163 us; the launch traced here: 162 us
  Pallas kernels  151 us (93%)
  local copies, waits for them, and re-layouts  10.8 us (7%)
    pallas_call x1, Pallas kernels, shards(): pl.pallas_call(kernel, out_shape=(token_out,) * 4 + (text_out,) * 2, in_s...  151 us
    unnamed x16, local copies, waits for them, and re-layouts  10.8 us

profile of v1, /device:TPU:6, one launch (start us, length us, event | category | flops | bytes accessed | tf_op | source)
XLA Modules:
  0.0 162.3 jit_solution(14285728259448495525)
XLA Ops:
  0.6 150.8 %shard_map.127 = (bf16[1,128,5120]{2,1,0:T(8,128)(2,1)}, bf16[1,128,5120]{2,1,0:T(8,128)(2,1)}, bf16[1,128,5120]{2,1,0:T(8,128)(2,1)}, bf16[1,128,5120]{2,1,0:T(...) custom-call(bf16[1,128,5120]{2,1,0:T(8,128)(2,1)} %sq.1, bf16[1,128,5120]{2,1,0:T(8,128)(2,1)} %sk.1, ...), custom_call_target="tpu_custom_call" | custom-call | flops 10737418240 | bytes 16777216 | tf_op jit(solution)/shard_map/pallas_call | solution.py:289
  151.5 0.0 copy-start.4
  151.5 2.6 %copy.20 = bf16[1,128,5120]{2,1,0:T(8,128)(2,1)} copy(bf16[1,128,5120]{2,1,0:T(8,128)(2,1)} %get-tuple-element.12) | data formatting | bytes 2621440
  154.1 0.0 copy-done.4
  154.1 0.0 copy-start.3
  154.1 1.1 copy.21
  155.1 0.7 copy-done.3
  155.8 0.0 copy-start.2
  155.8 1.1 copy.22
  156.9 0.7 copy-done.2
  157.6 0.0 copy-start.1
  157.6 1.1 copy.23
  158.7 0.7 copy-done.1
  159.4 0.0 copy-start
  159.4 1.1 copy.24
  160.5 0.7 copy-done
  161.2 1.1 copy.25
Async XLA Ops:
  151.5 2.6 %copy-start.4 = (bf16[1,128,5120]{2,1,0:T(8,128)(2,1)S(1)}, bf16[1,128,5120]{2,1,0:T(8,128)(2,1)}, u32[]{:S(2)}) copy-start(bf16[1,128,5120]{2,1,0:T(8,128)(2,1)} %get-tuple-element.13) | copy-start | bytes 3932164
  154.1 1.8 %copy-start.3 = (bf16[1,128,5120]{2,1,0:T(8,128)(2,1)S(1)}, bf16[1,128,5120]{2,1,0:T(8,128)(2,1)}, u32[]{:S(2)}) copy-start(bf16[1,128,5120]{2,1,0:T(8,128)(2,1)} %get-tuple-element.14) | copy-start | bytes 3932164
  155.8 1.8 %copy-start.2 = (bf16[1,128,5120]{2,1,0:T(8,128)(2,1)S(1)}, bf16[1,128,5120]{2,1,0:T(8,128)(2,1)}, u32[]{:S(2)}) copy-start(bf16[1,128,5120]{2,1,0:T(8,128)(2,1)} %get-tuple-element.15) | copy-start | bytes 3932164
  157.6 1.8 %copy-start.1 = (f32[512,640]{1,0:T(8,128)S(1)}, f32[512,640]{1,0:T(8,128)}, u32[]{:S(2)}) copy-start(f32[512,640]{1,0:T(8,128)} %get-tuple-element.16) | copy-start | bytes 3932164
  159.4 1.8 %copy-start = (f32[512,640]{1,0:T(8,128)S(1)}, f32[512,640]{1,0:T(8,128)}, u32[]{:S(2)}) copy-start(f32[512,640]{1,0:T(8,128)} %get-tuple-element.17) | copy-start | bytes 3932164

commit v2 on v1

--- a/solution.py
+++ b/solution.py
@@ -15,6 +15,9 @@
 SCALE = HD ** (-0.5)
 EXP2_SCALE = SCALE * math.log2(math.e)
 BLOCK = 256
+EARLY = 3
+LATE = 1
+STAGES = (1, 2, 3, 4)
 
 
 def contract(left, right, left_dim, right_dim):
@@ -41,20 +44,24 @@
 def kernel(
     sq, sk, sv, su, cq, ck, cv, cu,
     oq, ok, ov, ocq, ock, ocv,
-    self_in, cross_in, ctx, self_out, cross_out, part, pieces, turned, turned_in, other_in, gathered,
+    self_in, cross_in, ctx, self_out, cross_out, part, first, mid, second, turned, gathered,
     key_acc, value_acc,
     in_send, in_recv, x_send, x_recv, ctx_sem, o_send, o_recv, xo_send, xo_recv,
-    p_send, p_recv, t_send, t_recv, y_send, y_recv, g_send, g_recv,
+    a_send, a_recv, b_send, b_recv, t_send, t_recv, y_send, y_recv, g_send, g_recv,
 ):
     seq = lax.axis_index("seq")
     grp = lax.axis_index("grp")
     lane = lax.rem(grp, XC)
     row = lax.div(grp, XC)
+    along_z = lax.div(seq, 2)
+    high = lax.rem(seq, 2)
+    along_y = high * 2 + row
     heads = self_in.shape[0]
     tokens = sq.shape[1]
     rows = self_in.shape[2]
     text = part.shape[2]
-    text_piece = pieces.shape[3]
+    quarter = mid.shape[2]
+    piece = turned.shape[2]
 
     def seq_peer(d):
         return lax.rem(seq + d, SEQ)
@@ -68,17 +75,24 @@
     def at_lane(p):
         return {"seq": seq, "grp": row * XC + p}
 
+    def at_y(p):
+        return {"seq": along_z * 2 + lax.div(p, 2), "grp": lax.rem(p, 2) * XC + lane}
+
+    def at_z(p):
+        return {"seq": p * 2 + high, "grp": grp}
+
     turn_to = {"seq": lane, "grp": row * XC + seq}
     other_row = {"seq": seq, "grp": (1 - row) * XC + lane}
+    other_corner = {"seq": along_z * 2 + 1 - high, "grp": (1 - row) * XC + lane}
 
     def columns(owner, h):
         return pl.ds(pl.multiple_of((owner * heads + h) * HD, HD), HD)
 
+    def part_rows(owner, size):
+        return pl.ds(pl.multiple_of(owner * size, size), size)
+
     def token_rows(owner):
-        return pl.ds(pl.multiple_of(owner * tokens, tokens), tokens)
-
-    def text_rows(owner):
-        return pl.ds(pl.multiple_of(owner * text_piece, text_piece), text_piece)
+        return part_rows(owner, tokens)
 
     def remote(src, dst, send, recv, where):
         pltpu.make_async_remote_copy(
@@ -107,30 +121,39 @@
 
     lax.fori_loop(1, SEQ, greet, 0)
     pl.semaphore_signal(barrier, inc=1, device_id=other_row, device_id_type=MESH)
+    pl.semaphore_signal(barrier, inc=1, device_id=other_corner, device_id_type=MESH)
 
     @pl.when(lane != seq)
     def _():
         pl.semaphore_signal(barrier, inc=1, device_id=turn_to, device_id_type=MESH)
-        pl.semaphore_wait(barrier, SEQ + XC)
+        pl.semaphore_wait(barrier, SEQ + XC + 1)
 
     @pl.when(lane == seq)
     def _():
-        pl.semaphore_wait(barrier, SEQ + XC - 1)
-
-    def send_in(h, carry):
+        pl.semaphore_wait(barrier, SEQ + XC)
+
+    def send_cross(h, carry):
         for a, ref in enumerate((cq, cu)):
             local(ref.at[0, :, columns(lane, h)], cross_in.at[h, a, token_rows(lane)], x_recv.at[h])
-        for a, ref in enumerate((sq, sk, sv, su)):
-            local(ref.at[0, :, columns(seq, h)], self_in.at[h, a, token_rows(seq)], in_recv.at[h])
 
         def to_peer(d, inner):
-            p = seq_peer(d)
             e = lane_peer(d)
             for a, ref in enumerate((cq, cu)):
                 remote(
                     ref.at[0, :, columns(e, h)], cross_in.at[h, a, token_rows(lane)],
                     x_send, x_recv.at[h], at_lane(e),
                 )
+            return inner
+
+        lax.fori_loop(1, XC, to_peer, 0)
+        return carry
+
+    def send_self(h, carry):
+        for a, ref in enumerate((sq, sk, sv, su)):
+            local(ref.at[0, :, columns(seq, h)], self_in.at[h, a, token_rows(seq)], in_recv.at[h])
+
+        def to_peer(d, inner):
+            p = seq_peer(d)
             for a, ref in enumerate((sq, sk, sv, su)):
                 remote(
                     ref.at[0, :, columns(p, h)], self_in.at[h, a, token_rows(seq)],
@@ -141,7 +164,12 @@
         lax.fori_loop(1, SEQ, to_peer, 0)
         return carry
 
-    lax.fori_loop(0, heads, send_in, 0)
+    def send_both(h, carry):
+        send_cross(h, carry)
+        return send_self(h, carry)
+
+    lax.fori_loop(0, EARLY, send_both, 0)
+    lax.fori_loop(EARLY, heads, send_cross, 0)
 
     drain(ctx, ctx_sem)
 
@@ -164,24 +192,97 @@
         part[h, 0] = (key_acc[pl.ds(0, text), :] * SCALE).astype(jnp.bfloat16)
         part[h, 1] = value_acc[pl.ds(0, text), :].astype(jnp.bfloat16)
 
+        local(part.at[h, 0, part_rows(along_y, quarter)], first.at[0, along_y, h], a_recv)
+        local(part.at[h, 1, part_rows(along_z, quarter)], first.at[1, along_z, h], a_recv)
+
+        def to_quarter(d, inner):
+            p = lax.rem(along_y + d, 4)
+            remote(part.at[h, 0, part_rows(p, quarter)], first.at[0, along_y, h], a_send, a_recv, at_y(p))
+            p = lax.rem(along_z + d, 4)
+            remote(part.at[h, 1, part_rows(p, quarter)], first.at[1, along_z, h], a_send, a_recv, at_z(p))
+            return inner
+
+        lax.fori_loop(1, 4, to_quarter, 0)
+
         local(cross_out.at[h, token_rows(lane)], ocq.at[0, :, columns(lane, h)], xo_recv)
-        local(part.at[h, :, text_rows(seq)], pieces.at[seq, h], p_recv)
 
         def to_peer(d, inner):
-            p = seq_peer(d)
             e = lane_peer(d)
             remote(
                 cross_out.at[h, token_rows(e)], ocq.at[0, :, columns(lane, h)], xo_send, xo_recv, at_lane(e)
             )
-            remote(part.at[h, :, text_rows(p)], pieces.at[seq, h], p_send, p_recv, at_seq(p))
-            return inner
-
-        lax.fori_loop(1, SEQ, to_peer, 0)
+            return inner
+
+        lax.fori_loop(1, XC, to_peer, 0)
         return carry
 
     lax.fori_loop(0, heads, cross_head, 0)
 
+    def sum_quarters():
+        drain(first, a_recv)
+
+        def one(h, carry):
+            for a in range(2):
+                total = first[a, 0, h].astype(jnp.float32)
+                for i in range(1, 4):
+                    total = total + first[a, i, h].astype(jnp.float32)
+                mid[a, h] = total.astype(jnp.bfloat16)
+            return carry
+
+        lax.fori_loop(0, heads, one, 0)
+        local(mid.at[0, :, part_rows(along_z, piece)], second.at[0, along_z], b_recv)
+        local(mid.at[1, :, part_rows(along_y, piece)], second.at[1, along_y], b_recv)
+
+        def to_piece(d, carry):
+            p = lax.rem(along_z + d, 4)
+            remote(mid.at[0, :, part_rows(p, piece)], second.at[0, along_z], b_send, b_recv, at_z(p))
+            p = lax.rem(along_y + d, 4)
+            remote(mid.at[1, :, part_rows(p, piece)], second.at[1, along_y], b_send, b_recv, at_y(p))
+            return carry
+
+        lax.fori_loop(1, 4, to_piece, 0)
+
+    def sum_pieces():
+        drain(second, b_recv)
+        for a in range(2):
+            total = second[a, 0].astype(jnp.float32)
+            for i in range(1, 4):
+                total = total + second[a, i].astype(jnp.float32)
+            turned[a] = total.astype(jnp.bfloat16)
+
+        @pl.when(lane == seq)
+        def _():
+            local(turned, gathered.at[lane, row], t_recv)
+
+        @pl.when(lane != seq)
+        def _():
+            remote(turned, gathered.at[seq, row], t_send, t_recv, turn_to)
+
+    def share_rows():
+        drain(turned, t_recv)
+        remote(gathered.at[lane, row], gathered.at[lane, row], y_send, y_recv, other_row)
+
+    def share_lanes():
+        drain(turned, y_recv)
+
+        def to_lane(d, inner):
+            remote(gathered.at[lane], gathered.at[lane], g_send, g_recv, at_lane(lane_peer(d)))
+            return inner
+
+        lax.fori_loop(1, XC, to_lane, 0)
+
     def self_head(h, carry):
+        @pl.when(h == 0)
+        def _():
+            send_self(EARLY, 0)
+
+        for position, step in enumerate((sum_quarters, sum_pieces, share_rows, share_lanes)):
+            pl.when(h == STAGES[position])(step)
+
+        @pl.when(h == LATE)
+        def _():
+            send_self(EARLY + 1, 0)
+
         drain(self_in.at[h], in_recv.at[h])
         key_acc[...] = jnp.zeros_like(key_acc)
         value_acc[...] = jnp.zeros_like(value_acc)
@@ -213,60 +314,32 @@
             return inner
 
         lax.fori_loop(1, SEQ, to_peer, 0)
-
-        @pl.when(h == 1)
-        def _():
-            drain(pieces, p_recv)
-            total = pieces[0].astype(jnp.float32)
-            for i in range(1, SEQ):
-                total = total + pieces[i].astype(jnp.float32)
-            turned[...] = total
-
-            @pl.when(lane == seq)
-            def _():
-                local(turned, turned_in, t_recv)
-
-            @pl.when(lane != seq)
-            def _():
-                remote(turned, turned_in, t_send, t_recv, turn_to)
-
-        @pl.when(h == 2)
-        def _():
-            drain(turned_in, t_recv)
-            remote(turned_in, other_in, y_send, y_recv, other_row)
-
-        @pl.when(h == 3)
-        def _():
-            drain(other_in, y_recv)
-            gathered[lane] = (turned_in[...] + other_in[...]).astype(jnp.bfloat16)
-
-            def to_lane(d, inner):
-                remote(gathered.at[lane], gathered.at[lane], g_send, g_recv, at_lane(lane_peer(d)))
-                return inner
-
-            lax.fori_loop(1, XC, to_lane, 0)
-
         return carry
 
     lax.fori_loop(0, heads, self_head, 0)
 
     drain(gathered.at[pl.ds(0, XC - 1)], g_recv)
     for h in range(heads):
-        for j in range(XC):
-            ock[pl.ds(j * text_piece, text_piece), pl.ds(h * HD, HD)] = gathered[j, h, 0].astype(jnp.float32)
-            ocv[pl.ds(j * text_piece, text_piece), pl.ds(h * HD, HD)] = gathered[j, h, 1].astype(jnp.float32)
+        at = pl.ds(h * HD, HD)
+        for e in range(XC):
+            z, y_high = divmod(e, 2)
+            for r in range(2):
+                y = y_high * 2 + r
+                ock[pl.ds(y * quarter + z * piece, piece), at] = gathered[e, r, 0, h].astype(jnp.float32)
+                ocv[pl.ds(z * quarter + y * piece, piece), at] = gathered[e, r, 1, h].astype(jnp.float32)
 
     others = rows - tokens
     drain(self_in.at[:, :, pl.ds(0, others)], in_send)
     drain(cross_in.at[:, :, pl.ds(0, others)], x_send)
     drain(cross_out.at[:, pl.ds(0, others)], xo_send)
-    drain(pieces.at[pl.ds(0, SEQ - 1)], p_send)
+    drain(first.at[:, pl.ds(0, 3)], a_send)
+    drain(second.at[:, pl.ds(0, 3)], b_send)
 
     @pl.when(lane != seq)
     def _():
         drain(turned, t_send)
 
-    drain(turned_in, y_send)
+    drain(turned, y_send)
     drain(gathered.at[pl.ds(0, XC - 1)], g_send)
     drain(self_out.at[:, :, pl.ds(0, others)], o_send)
     drain(ocq, xo_recv)
@@ -274,23 +347,34 @@
         drain(ref, o_recv.at[a])
 
 
+def to_hbm(*refs):
+    count = len(refs) // 2
+    sems = refs[-1]
+    copies = [pltpu.make_async_copy(refs[i], refs[count + i], sems.at[i]) for i in range(count)]
+    for copy in copies:
+        copy.start()
+    for copy in copies:
+        copy.wait()
+
+
 def shards(sq, sk, sv, su, cq, ck, cv, cu):
     tokens, width = sq.shape[1], sq.shape[2]
     text = ck.shape[0]
     rows = tokens * SEQ
     heads = width // HD // SEQ
-    piece = text // SEQ
+    quarter, piece = text // 4, text // 16
     half, full = jnp.bfloat16, jnp.float32
-    token_out = jax.ShapeDtypeStruct((1, tokens, width), half)
-    text_out = jax.ShapeDtypeStruct((text, width // SEQ), full)
+    token_shape = ((1, tokens, width), half)
+    text_shape = ((text, width // SEQ), full)
+    out_shapes = (token_shape,) * 4 + (text_shape,) * 2
     in_any = pl.BlockSpec(memory_space=pl.ANY)
     in_vmem = pl.BlockSpec(memory_space=pltpu.VMEM)
     dma = pltpu.SemaphoreType.DMA
-    return pl.pallas_call(
+    results = pl.pallas_call(
         kernel,
-        out_shape=(token_out,) * 4 + (text_out,) * 2,
+        out_shape=tuple(pltpu.VMEM(*shape) for shape in out_shapes),
         in_specs=[in_any] * 8,
-        out_specs=(in_any,) * 4 + (in_vmem,) * 2,
+        out_specs=(in_vmem,) * 6,
         scratch_shapes=[
             pltpu.VMEM((heads, 4, rows, HD), half),
             pltpu.VMEM((heads, 2, rows, HD), half),
@@ -298,21 +382,29 @@
             pltpu.VMEM((heads, 3, rows, HD), half),
             pltpu.VMEM((heads, rows, HD), half),
             pltpu.VMEM((heads, 2, text, HD), half),
-            pltpu.VMEM((SEQ, heads, 2, piece, HD), half),
-            pltpu.VMEM((heads, 2, piece, HD), full),
-            pltpu.VMEM((heads, 2, piece, HD), full),
-            pltpu.VMEM((heads, 2, piece, HD), full),
-            pltpu.VMEM((XC, heads, 2, piece, HD), half),
+            pltpu.VMEM((2, 4, heads, quarter, HD), half),
+            pltpu.VMEM((2, heads, quarter, HD), half),
+            pltpu.VMEM((2, 4, heads, piece, HD), half),
+            pltpu.VMEM((2, heads, piece, HD), half),
+            pltpu.VMEM((XC, 2, 2, heads, piece, HD), half),
             pltpu.VMEM((rows, HD), full),
             pltpu.VMEM((rows, HD), full),
             dma, dma((heads,)), dma, dma((heads,)), dma, dma, dma((3,)), dma, dma,
-            dma, dma, dma, dma, dma, dma, dma, dma,
+            dma, dma, dma, dma, dma, dma, dma, dma, dma, dma,
         ],
         compiler_params=pltpu.CompilerParams(
-            collective_id=0, has_side_effects=True, vmem_limit_bytes=58 << 20
+            collective_id=0, has_side_effects=True, vmem_limit_bytes=46 << 20
         ),
         cost_estimate=pl.CostEstimate(flops=10 << 30, bytes_accessed=16 << 20, transcendentals=8 << 20),
     )(sq, sk, sv, su, cq, ck, cv, cu)
+    return pl.pallas_call(
+        to_hbm,
+        out_shape=tuple(jax.ShapeDtypeStruct(*shape) for shape in out_shapes),
+        in_specs=[in_vmem] * 6,
+        out_specs=(in_any,) * 6,
+        scratch_shapes=[dma((6,))],
+        compiler_params=pltpu.CompilerParams(vmem_limit_bytes=1 << 20),
+    )(*results)
 
 
 def solution(mesh):

time: 163 us -> 131 us (0.80)
  the two profiles are of different devices: /device:TPU:6 before, /device:TPU:85 now
where the time goes in v2:
time: 131 us
  Pallas kernels  130 us (99%)
    pallas_call x1, Pallas kernels, shards(): pl.pallas_call(kernel, out_shape=tuple((pltpu.VMEM(*shape) for shape in o...  127 us
    pallas_call x1, Pallas kernels, shards(): pl.pallas_call(to_hbm, out_shape=tuple((jax.ShapeDtypeStruct(*shape) for...  3.23 us

profile of v2, /device:TPU:85, one launch (start us, length us, event | category | flops | bytes accessed | tf_op | source)
XLA Modules:
  0.0 130.6 jit_solution(15331700431101524520)
XLA Ops:
  0.6 126.7 %shard_map.127 = (bf16[1,128,5120]{2,1,0:T(8,128)(2,1)S(1)}, bf16[1,128,5120]{2,1,0:T(8,128)(2,1)S(1)}, bf16[1,128,5120]{2,1,0:T(8,128)(2,1)S(1)}, bf16[1,128,51...) custom-call(bf16[1,128,5120]{2,1,0:T(8,128)(2,1)} %sq.1, bf16[1,128,5120]{2,1,0:T(8,128)(2,1)} %sk.1, ...), custom_call_target="tpu_custom_call" | custom-call | flops 10737418240 | bytes 16777216 | tf_op jit(solution)/shard_map/pallas_call | solution.py:373
  127.4 3.2 %shard_map.128 = (bf16[1,128,5120]{2,1,0:T(8,128)(2,1)}, bf16[1,128,5120]{2,1,0:T(8,128)(2,1)}, bf16[1,128,5120]{2,1,0:T(8,128)(2,1)}, bf16[1,128,5120]{2,1,0:T(...) custom-call(bf16[1,128,5120]{2,1,0:T(8,128)(2,1)S(1)} %get-tuple-element.12.refs_0_, ...), custom_call_target="tpu_custom_call" | custom-call | tf_op jit(solution)/shard_map/pallas_call | solution.py:400

commit v3 on v2

--- a/solution.py
+++ b/solution.py
@@ -15,6 +15,7 @@
 SCALE = HD ** (-0.5)
 EXP2_SCALE = SCALE * math.log2(math.e)
 BLOCK = 256
+CHUNKS = 4
 EARLY = 3
 LATE = 1
 STAGES = (1, 2, 3, 4)
@@ -64,7 +65,8 @@
     piece = turned.shape[2]
 
     def seq_peer(d):
-        return lax.rem(seq + d, SEQ)
+        d = lax.rem(d - 1 + lax.rem(lane, 2) * 3, SEQ - 1) + 1
+        return lax.rem(along_z + lax.div(d, 2), 4) * 2 + lax.rem(high + lax.rem(d, 2), 2)
 
     def lane_peer(d):
         return lax.rem(lane + d, XC)
@@ -149,8 +151,6 @@
         return carry
 
     def send_self(h, carry):
-        for a, ref in enumerate((sq, sk, sv, su)):
-            local(ref.at[0, :, columns(seq, h)], self_in.at[h, a, token_rows(seq)], in_recv.at[h])
 
         def to_peer(d, inner):
             p = seq_peer(d)
@@ -162,11 +162,13 @@
             return inner
 
         lax.fori_loop(1, SEQ, to_peer, 0)
+        for a, ref in enumerate((sq, sk, sv, su)):
+            local(ref.at[0, :, columns(seq, h)], self_in.at[h, a, token_rows(seq)], in_recv.at[h])
         return carry
 
     def send_both(h, carry):
-        send_cross(h, carry)
-        return send_self(h, carry)
+        send_self(h, carry)
+        return send_cross(h, carry)
 
     lax.fori_loop(0, EARLY, send_both, 0)
     lax.fori_loop(EARLY, heads, send_cross, 0)
@@ -350,7 +352,12 @@
 def to_hbm(*refs):
     count = len(refs) // 2
     sems = refs[-1]
-    copies = [pltpu.make_async_copy(refs[i], refs[count + i], sems.at[i]) for i in range(count)]
+    copies = []
+    for i in range(count):
+        rows = refs[i].shape[-2] // CHUNKS
+        for j in range(CHUNKS):
+            at = (0,) * (len(refs[i].shape) - 2) + (pl.ds(j * rows, rows),)
+            copies.append(pltpu.make_async_copy(refs[i].at[at], refs[count + i].at[at], sems.at[i, j]))
     for copy in copies:
         copy.start()
     for copy in copies:
@@ -402,7 +409,7 @@
         out_shape=tuple(jax.ShapeDtypeStruct(*shape) for shape in out_shapes),
         in_specs=[in_vmem] * 6,
         out_specs=(in_any,) * 6,
-        scratch_shapes=[dma((6,))],
+        scratch_shapes=[dma((6, CHUNKS))],
         compiler_params=pltpu.CompilerParams(vmem_limit_bytes=1 << 20),
     )(*results)
 

time: 131 us -> 127 us (0.969)
  the two profiles are of different devices: /device:TPU:85 before, /device:TPU:1 now
where the time goes in v3:
time: 127 us; the launch traced here: 126 us
  Pallas kernels  125 us (98%)
    pallas_call x1, Pallas kernels, shards(): pl.pallas_call(kernel, out_shape=tuple((pltpu.VMEM(*shape) for shape in o...  122 us
    pallas_call x1, Pallas kernels, shards(): pl.pallas_call(to_hbm, out_shape=tuple((jax.ShapeDtypeStruct(*shape) for...  3.32 us

profile of v3, /device:TPU:1, one launch (start us, length us, event | category | flops | bytes accessed | tf_op | source)
XLA Modules:
  0.0 125.6 jit_solution(3592425288262172139)
XLA Ops:
  0.6 121.6 %shard_map.127 = (bf16[1,128,5120]{2,1,0:T(8,128)(2,1)S(1)}, bf16[1,128,5120]{2,1,0:T(8,128)(2,1)S(1)}, bf16[1,128,5120]{2,1,0:T(8,128)(2,1)S(1)}, bf16[1,128,51...) custom-call(bf16[1,128,5120]{2,1,0:T(8,128)(2,1)} %sq.1, bf16[1,128,5120]{2,1,0:T(8,128)(2,1)} %sk.1, ...), custom_call_target="tpu_custom_call" | custom-call | flops 10737418240 | bytes 16777216 | tf_op jit(solution)/shard_map/pallas_call | solution.py:380
  122.2 3.3 %shard_map.128 = (bf16[1,128,5120]{2,1,0:T(8,128)(2,1)}, bf16[1,128,5120]{2,1,0:T(8,128)(2,1)}, bf16[1,128,5120]{2,1,0:T(8,128)(2,1)}, bf16[1,128,5120]{2,1,0:T(...) custom-call(bf16[1,128,5120]{2,1,0:T(8,128)(2,1)S(1)} %get-tuple-element.12.refs_0_, ...), custom_call_target="tpu_custom_call" | custom-call | tf_op jit(solution)/shard_map/pallas_call | solution.py:407

commit v4 on v3

--- a/solution.py
+++ b/solution.py
@@ -83,7 +83,12 @@
     def at_z(p):
         return {"seq": p * 2 + high, "grp": grp}
 
-    turn_to = {"seq": lane, "grp": row * XC + seq}
+    core = lax.rem(lane, 2)
+    turn_to = {"seq": lane, "grp": row * XC + lax.rem(seq + lane - core, SEQ)}
+    held = lax.rem(lane - seq + high + SEQ, SEQ)
+    turn_from = {"seq": held, "grp": row * XC + seq}
+    stays = (lane == seq) & (seq == core)
+    moves = (lane != seq) | (seq != core)
     other_row = {"seq": seq, "grp": (1 - row) * XC + lane}
     other_corner = {"seq": along_z * 2 + 1 - high, "grp": (1 - row) * XC + lane}
 
@@ -125,12 +130,13 @@
     pl.semaphore_signal(barrier, inc=1, device_id=other_row, device_id_type=MESH)
     pl.semaphore_signal(barrier, inc=1, device_id=other_corner, device_id_type=MESH)
 
-    @pl.when(lane != seq)
+    @pl.when(moves)
     def _():
         pl.semaphore_signal(barrier, inc=1, device_id=turn_to, device_id_type=MESH)
-        pl.semaphore_wait(barrier, SEQ + XC + 1)
-
-    @pl.when(lane == seq)
+        pl.semaphore_signal(barrier, inc=1, device_id=turn_from, device_id_type=MESH)
+        pl.semaphore_wait(barrier, SEQ + XC + 2)
+
+    @pl.when(stays)
     def _():
         pl.semaphore_wait(barrier, SEQ + XC)
 
@@ -252,23 +258,23 @@
                 total = total + second[a, i].astype(jnp.float32)
             turned[a] = total.astype(jnp.bfloat16)
 
-        @pl.when(lane == seq)
+        @pl.when(stays)
         def _():
-            local(turned, gathered.at[lane, row], t_recv)
-
-        @pl.when(lane != seq)
+            local(turned, gathered.at[seq, row], t_recv)
+
+        @pl.when(moves)
         def _():
             remote(turned, gathered.at[seq, row], t_send, t_recv, turn_to)
 
     def share_rows():
         drain(turned, t_recv)
-        remote(gathered.at[lane, row], gathered.at[lane, row], y_send, y_recv, other_row)
+        remote(gathered.at[held, row], gathered.at[held, row], y_send, y_recv, other_row)
 
     def share_lanes():
         drain(turned, y_recv)
 
         def to_lane(d, inner):
-            remote(gathered.at[lane], gathered.at[lane], g_send, g_recv, at_lane(lane_peer(d)))
+            remote(gathered.at[held], gathered.at[held], g_send, g_recv, at_lane(lane_peer(d)))
             return inner
 
         lax.fori_loop(1, XC, to_lane, 0)
@@ -337,7 +343,7 @@
     drain(first.at[:, pl.ds(0, 3)], a_send)
     drain(second.at[:, pl.ds(0, 3)], b_send)
 
-    @pl.when(lane != seq)
+    @pl.when(moves)
     def _():
         drain(turned, t_send)
 

time: 127 us -> 126 us (level)
  no operation moved by 1% of the time
where the time goes in v4:
time: 126 us; the launch traced here: 125 us
  Pallas kernels  125 us (99%)
    pallas_call x1, Pallas kernels, shards(): pl.pallas_call(kernel, out_shape=tuple((pltpu.VMEM(*shape) for shape in o...  122 us
    pallas_call x1, Pallas kernels, shards(): pl.pallas_call(to_hbm, out_shape=tuple((jax.ShapeDtypeStruct(*shape) for...  3.32 us

profile of v4, /device:TPU:1, one launch (start us, length us, event | category | flops | bytes accessed | tf_op | source)
XLA Modules:
  0.0 125.5 jit_solution(16024108444827531368)
XLA Ops:
  0.6 121.5 %shard_map.127 = (bf16[1,128,5120]{2,1,0:T(8,128)(2,1)S(1)}, bf16[1,128,5120]{2,1,0:T(8,128)(2,1)S(1)}, bf16[1,128,5120]{2,1,0:T(8,128)(2,1)S(1)}, bf16[1,128,51...) custom-call(bf16[1,128,5120]{2,1,0:T(8,128)(2,1)} %sq.1, bf16[1,128,5120]{2,1,0:T(8,128)(2,1)} %sk.1, ...), custom_call_target="tpu_custom_call" | custom-call | flops 10737418240 | bytes 16777216 | tf_op jit(solution)/shard_map/pallas_call | solution.py:386
  122.2 3.3 %shard_map.128 = (bf16[1,128,5120]{2,1,0:T(8,128)(2,1)}, bf16[1,128,5120]{2,1,0:T(8,128)(2,1)}, bf16[1,128,5120]{2,1,0:T(8,128)(2,1)}, bf16[1,128,5120]{2,1,0:T(...) custom-call(bf16[1,128,5120]{2,1,0:T(8,128)(2,1)S(1)} %get-tuple-element.12.refs_0_, ...), custom_call_target="tpu_custom_call" | custom-call | tf_op jit(solution)/shard_map/pallas_call | solution.py:413
